TPU v7x, 1024 devices: a whole 4x4x32 slice. The times are simulated.
1024 devices in a mesh: dp: 128 (over z, y), opt: 8 (over x, core).
Axes of the slice: x: 4, y: 4, z: 32, core: 2. Of those that a mesh axis runs over, the one named last changes fastest.
Arguments:
- activations: bfloat16 [262144, 1024], P(('dp', 'opt')), may hold values from -24 to 24
- hidden_grad: bfloat16 [262144, 8, 384], P(('dp', 'opt')), may hold values from -6 to 6
- routing: int32 [262144, 8], P(('dp', 'opt')), may hold values from 0 to 127, all different within a row; in each aligned block of 256 rows (0 to 255, 256 to 511, ...) at most 32 rows name the same one
- momentum: float32 [8, 1024, 384], P('opt', 'dp'), may hold values from -600 to 600
- master: float32 [8, 1024, 384], P('opt', 'dp'), may hold values from -6 to 6
Outputs:
- momentum_out: float32 [8, 1024, 384], P('opt', 'dp')
- master_out: float32 [8, 1024, 384], P('opt', 'dp')
- update: float32 [8, 1024, 384], P('opt', 'dp')
Inputs may be any that keep to these rules, and one draw needn't show every extreme that they name: `routing`: each row names 8 different experts. Among the 256 rows of one device, at most 32 name any one expert.
All inputs are finite; a program needn't handle non-finite values.
Results may differ from a plain program's by a relative error of at most 0.0006.
Values may be sent and summed in bfloat16 or wider, within the bound.
A program may use at most 32 MiB of HBM per device.

v0:
```python
import math

import jax
import jax.numpy as jnp
from jax import lax
from jax.sharding import PartitionSpec as P

ITERS = 2
CAP = 32


poly_first = 3.4445
poly_third = -4.775
poly_fifth = 2.0315
momentum_decay = 0.95
learning_rate = 0.02
weight_decay = 0.1
norm_epsilon = 1e-07


def inner_gram(first_side, second_side):
    return lax.dot_general(
        first_side,
        second_side,
        (((0,), (0,)), ((), ())),
        precision=lax.Precision.HIGHEST,
        preferred_element_type=jnp.float32,
    )


def matmul_exact(first_side, second_side):
    return jnp.dot(
        first_side, second_side, precision=lax.Precision.HIGHEST, preferred_element_type=jnp.float32
    )


def newton_step(iterate, gram_now):
    polynomial = poly_third * gram_now + poly_fifth * matmul_exact(gram_now, gram_now)
    return poly_first * iterate + matmul_exact(iterate, polynomial)


def pack_rows(activations, hidden_grad, routing, expert):
    tok_count = activations.shape[0]
    matched = routing == expert
    chosen = jnp.any(matched, axis=1)
    order_key = jnp.where(chosen, 0, tok_count).astype(jnp.int32) + jnp.arange(
        tok_count, dtype=jnp.int32
    )
    picked = jnp.argsort(order_key)[:CAP]
    picked_acts = activations[picked]
    selected_grad = jnp.where(
        matched[picked][:, :, None], hidden_grad[picked], jnp.zeros((), hidden_grad.dtype)
    )
    picked_grads = jnp.sum(selected_grad, axis=1)
    return (picked_acts, picked_grads)


def per_device(activations, hidden_grad, routing, momentum, master):
    groups = lax.axis_size("opt")
    experts = jnp.arange(groups, dtype=jnp.int32)
    packed_acts, packed_grads = jax.vmap(
        lambda expert: pack_rows(activations, hidden_grad, routing, expert)
    )(experts)
    got_acts, got_grads = (
        lax.all_to_all(packed_acts, "opt", split_axis=0, concat_axis=0, tiled=True),
        lax.all_to_all(packed_grads, "opt", split_axis=0, concat_axis=0, tiled=True),
    )
    model_width = activations.shape[1]
    hidden = hidden_grad.shape[2]
    flat_acts = got_acts.reshape(-1, model_width)
    flat_grads = got_grads.reshape(-1, hidden)
    shard_rows = model_width // lax.axis_size("dp")
    grad_shard = lax.psum_scatter(
        lax.dot_general(
            flat_acts, flat_grads, (((0,), (0,)), ((), ())), preferred_element_type=jnp.float32
        ),
        "dp",
        scatter_dimension=0,
        tiled=True,
    )
    new_moment = momentum_decay * momentum[0] + grad_shard
    matrix = lax.all_gather(new_moment, "dp", axis=0, tiled=True)
    first_gram = inner_gram(matrix, matrix)
    norm_scale = lax.rsqrt(jnp.trace(first_gram) + norm_epsilon)
    iterate = matrix * norm_scale
    gram_now = first_gram * (norm_scale * norm_scale)
    for step_index in range(ITERS):
        if step_index > 0:
            gram_now = inner_gram(iterate, iterate)
        iterate = newton_step(iterate, gram_now)
    own_rows = lax.dynamic_slice_in_dim(iterate, lax.axis_index("dp") * shard_rows, shard_rows, 0)
    update = 0.2 * math.sqrt(max(model_width, hidden)) * own_rows
    master_out = (1.0 - learning_rate * weight_decay) * master[0] - learning_rate * update
    return (new_moment[None], master_out[None], update[None])


def solution(mesh):
    placed = (
        P(("dp", "opt"), None),
        P(("dp", "opt"), None, None),
        P(("dp", "opt"), None),
        P("opt", "dp", None),
        P("opt", "dp", None),
    )
    return jax.shard_map(
        per_device,
        mesh=mesh,
        in_specs=placed,
        out_specs=(P("opt", "dp", None), P("opt", "dp", None), P("opt", "dp", None)),
        check_vma=False,
    )
```

profile of v0, /device:TPU:2, one launch (start us, length us, event | category | flops | bytes accessed | tf_op | source)
XLA Modules:
  0.0 853.5 jit_solution(12617829194380743911)
XLA Ops:
  7.2 0.0 copy-start
  7.2 0.0 sort.19.cloned.1.call-start
  7.2 0.9 copy.9
  8.2 0.4 iota_compare_fusion
  8.5 0.6 iota_add_fusion
  9.1 0.6 broadcast_in_dim.48
  9.7 0.0 sort.19.cloned.1.call-update
  9.8 4.0 sort.19.cloned.1.call-done
  13.7 0.7 compare_select_fusion
  14.4 0.7 bitcast_or_fusion
  15.1 0.1 reshape.16
  15.2 0.1 reshape.30
  15.3 0.0 copy-done
  15.3 2.0 gather_fusion.1
  17.3 0.0 copy-start.1
  17.3 1.6 gather_fusion.2
  18.9 3.0 select_reduce_fusion
  21.9 16.5 %all-to-all-start.1 = ((bf16[8,32,384]{2,1,0:T(8,128)(2,1)}), bf16[8,32,384]{2,1,0:T(8,128)(2,1)S(1)}, u32[]{:S(2)}, u32[]{:S(2)}) async-start(bf16[8,32,384]{2,1,0:T(8,128)(2,1)} %select_reduce_fusion), calls=%async_computation.1 | async-start | bytes 393216 | tf_op jit(solution)/shard_map/all_to_all | solution.py:66
  38.4 0.0 all-reduce.3.cloned.1.call-start
  38.4 0.0 copy-done.1
  38.4 1.2 gather_fusion
  39.5 4.2 all-to-all-done.1
  43.8 12.8 %all_to_all.10 = bf16[8,32,1024]{2,1,0:T(8,128)(2,1)S(1)} all-to-all(bf16[8,32,1024]{2,1,0:T(8,128)(2,1)S(1)} %bitcast.33), channel_id=1, replica_groups=mesh['dp'=128,'opt'=8] {'opt'}, dimensions={0} | all-to-all | bytes 1048576 | tf_op jit(solution)/shard_map/all_to_all | solution.py:65
  56.6 1.6 convolution_bitcast_fusion
  58.2 0.0 copy-start.3
  58.2 0.0 all-reduce.3.cloned.1.call-update
  58.2 0.2 all-gather.2.cloned.1.call-start
  58.4 1.3 dynamic-slice
  60.4 505.8 %all-reduce.3.cloned.1.call-done = f32[1024,384]{1,0:T(8,128)} async-done(((f32[1024,384]{1,0:T(8,128)}), f32[1024,384]{1,0:T(8,128)}) %all-reduce.3.cloned.1.call-update) | async-done | bytes 1572880
  566.1 0.0 copy-done.3
  566.1 1.3 dynamic-slice_add_fusion.1
  567.4 0.0 all-gather.2.cloned.1.call-update
  567.5 258.7 %all-gather.2.cloned.1.call-done = f32[1024,384]{1,0:T(8,128)} async-done(((f32[8,384]{1,0:T(8,128)}), f32[1024,384]{1,0:T(8,128)}) %all-gather.2.cloned.1.call-update) | async-done | bytes 1572880 | tf_op jit(solution)/shard_map/all_gather | solution.py:82
  826.2 0.0 copy-start.2
  826.2 6.1 select_reduce_fusion.1
  833.0 2.8 fusion.1
  835.8 0.0 copy-done.2
  835.8 3.2 multiply_add_fusion
  839.0 2.8 fusion.8
  841.8 1.3 fusion.2
  843.1 0.0 copy-start.4
  843.1 3.3 fusion.9
  846.4 0.0 copy-done.4
  846.4 0.6 multiply_bitcast_fusion
  (1 shorter events, 0.0 us)
Async XLA Ops:
  7.2 8.1 copy-start
  7.2 6.5 sort.19.cloned.1.call-start
  17.3 21.1 %copy-start.1 = (bf16[256,1024]{1,0:T(8,128)(2,1)S(1)}, bf16[256,1024]{1,0:T(8,128)(2,1)}, u32[]{:S(2)}) copy-start(bf16[256,1024]{1,0:T(8,128)(2,1)} %param.5) | copy-start | bytes 1572868
  21.9 21.9 %all-to-all-start.1 = ((bf16[8,32,384]{2,1,0:T(8,128)(2,1)}), bf16[8,32,384]{2,1,0:T(8,128)(2,1)S(1)}, u32[]{:S(2)}, u32[]{:S(2)}) async-start(bf16[8,32,384]{2,1,0:T(8,128)(2,1)} %select_reduce_fusion), calls=%async_computation.1 | async-start | bytes 393216 | tf_op jit(solution)/shard_map/all_to_all | solution.py:66
  38.4 527.8 %all-reduce.3.cloned.1.call-start = ((), (), s32[]{:S(2)}) async-start(), calls=%async_computation.3 | async-start | bytes 3145728
  58.2 507.9 %copy-start.3 = (f32[1,8,384]{2,1,0:T(8,128)S(1)}, f32[1,8,384]{2,1,0:T(8,128)}, u32[]{:S(2)}) copy-start(f32[1,8,384]{2,1,0:T(8,128)} %param.8) | copy-start | bytes 36868
  58.2 768.0 %all-gather.2.cloned.1.call-start = ((), (), s32[]{:S(2)}) async-start(), calls=%async_computation.2 | async-start | bytes 1585152 | tf_op jit(solution)/shard_map/all_gather | solution.py:82
  826.2 9.6 %copy-start.2 = (f32[1024,384]{1,0:T(8,128)S(1)}, f32[1024,384]{1,0:T(8,128)}, u32[]{:S(2)}) copy-start(f32[1024,384]{1,0:T(8,128)} %all-gather.2.cloned.1.call-done) | copy-start | bytes 4718596
  843.1 3.3 copy-start.4
Sparse Core Ops, SparseCore 0:
  10.9 2.4 sort.21.cloned.1.call-done
  58.3 507.7 all-reduce.2
  570.8 255.3 all-gather.1
  (1 shorter events, 0.0 us)
where the time goes:
time: 854 us
  waiting for transfers between devices  769 us (90%)
  matrix products  21.1 us (2%)
  starting transfers between devices  16.7 us (2%)
  between operations  15.2 us (2%)
  blocking collectives  12.8 us (1%)
  local copies, waits for them, and re-layouts  11.8 us (1%)
    unnamed x3, waiting for transfers between devices  506 us
    all_gather x1, waiting for transfers between devices, per_device(): matrix = lax.all_gather(new_moment, 'dp', axis=0, tiled=True)  259 us
  transfers between devices with their start and end apart: 3, of which 3 were waited for; matrix products, arithmetic and copies ran while one was open for 0% of the time, Pallas kernels for 0%

commit v1 on v0

v1 whole, which is shorter than its diff:
```python
import functools
import math

import jax
import jax.numpy as jnp
from jax import lax
from jax.experimental import pallas as pl
from jax.experimental.pallas import tpu as pltpu
from jax.sharding import PartitionSpec as P

CAP = 32
NY = 4
INNER = 4
STRIDE = 11
MESH = pl.DeviceIdType.MESH

poly_first = 3.4445
poly_third = -4.775
poly_fifth = 2.0315
momentum_decay = 0.95
learning_rate = 0.02
weight_decay = 0.1
norm_epsilon = 1e-07

f32 = jnp.float32
bf16 = jnp.bfloat16


def halves(a):
    hi = a.astype(bf16)
    return hi, (a - hi.astype(f32)).astype(bf16)


def dot(a, b):
    return jnp.dot(a, b, preferred_element_type=f32)


def dot_t(a, b):
    return lax.dot_general(a, b, (((0,), (0,)), ((), ())), preferred_element_type=f32)


def dot3(a, b):
    (a_hi, a_lo), (b_hi, b_lo) = a, b
    return dot(a_hi, b_hi) + (dot(a_hi, b_lo) + dot(a_lo, b_hi))


def one_hot(cond):
    return jnp.where(cond, 1.0, 0.0).astype(bf16)


def running_count(flags):
    width = flags.shape[1]
    lane = lax.broadcasted_iota(jnp.int32, flags.shape, 1)
    total, shift = flags, 1
    while shift < width:
        total = total + jnp.where(lane >= shift, pltpu.roll(total, shift, 1), 0)
        shift *= 2
    return total


OFFSETS = (0, 1, 7, 2, 6, 3, 5, 4)
GROUPS = ((0, 3), (3, 5), (5, 8))


def kernel(
    sizes,
    acts_hbm, hidden_hbm, names_hbm, momentum_hbm, master_hbm,
    moment_out, master_out, update_out,
    acts, hidden, names, momentum, master,
    pick, send, recv, part, near, summed, far, rows,
    load_sem, local_sem, know_four, know_eight,
    go_send, go_recv, near_send, near_recv, far_send, far_recv,
    out_send, out_recv, around_send, around_recv, side_send, side_recv,
):
    nz, n_opt = sizes
    outer = nz // INNER
    dp, opt = lax.axis_index("dp"), lax.axis_index("opt")
    z, y = dp // NY, dp % NY
    cls, place = z % INNER, z // INNER
    width = acts.shape[1]
    quarter = width // NY
    hid = hidden.shape[1]
    group = NY * n_opt

    def at(zz, yy, oo):
        return (zz * NY + yy, oo)

    def offsets(i):
        r = i * STRIDE % group
        return r // n_opt, r % n_opt

    def go_peer(i):
        dy, do = offsets(i)
        return at(z, (y + dy) % NY, (opt + do) % n_opt)

    def go_source(i):
        dy, do = offsets(i)
        return at(z, (y + NY - dy) % NY, (opt + n_opt - do) % n_opt)

    def along(dz):
        return at((z + nz + dz) % nz, y, opt)

    even = 1 - z % 2
    turn = 2 * even - (1 - even) * 2
    near_to = [along(1), along(-1), along(turn)]

    def far_to(q):
        return at((place + q) % outer * INNER + cls, y, opt)

    barrier = pltpu.get_barrier_semaphore()

    def greet(i, _):
        pl.semaphore_signal(barrier, inc=1, device_id=go_source(i), device_id_type=MESH)
        return 0

    loads = [
        pltpu.make_async_copy(source, target, load_sem.at[i])
        for i, (source, target) in enumerate(
            [
                (names_hbm, names),
                (acts_hbm, acts),
                (hidden_hbm, hidden),
                (momentum_hbm, momentum),
                (master_hbm, master),
            ]
        )
    ]
    for load in loads:
        load.start()
    lax.fori_loop(1, group, greet, 0)
    for dz in (1, -1, 2, -2, 4, -4):
        pl.semaphore_signal(barrier, inc=1, device_id=along(dz), device_id_type=MESH)

    experts, tokens, top = n_opt, acts.shape[0], names.shape[0]
    spread_shape = (tokens, tokens * top)
    spread = one_hot(
        (lax.broadcasted_iota(jnp.int32, spread_shape, 1) >> (top.bit_length() - 1))
        == lax.broadcasted_iota(jnp.int32, spread_shape, 0)
    )
    loads[0].wait()
    expert = lax.broadcasted_iota(jnp.int32, (experts, tokens), 0)
    match = jnp.zeros((experts, tokens), jnp.int32)
    for k in range(top):
        match = match + (names[k : k + 1, :] == expert).astype(jnp.int32)
    per_token = jnp.where(match > 0, running_count(match) - 1, -1)
    both = jnp.concatenate([names[...], per_token], axis=0).astype(f32).astype(bf16)
    wide = dot(both, spread)
    slot = lax.broadcasted_iota(jnp.int32, (top, tokens * top), 1) & (top - 1)
    own_slot = slot == lax.broadcasted_iota(jnp.int32, slot.shape, 0)
    name = jnp.sum(jnp.where(own_slot, wide[:top], 0.0), axis=0, keepdims=True)
    expert = lax.broadcasted_iota(jnp.int32, (experts, tokens * top), 0).astype(f32)
    flat = jnp.where(name == expert, wide[top:], -1.0)
    for e in range(experts):
        j = lax.broadcasted_iota(jnp.int32, (CAP, flat.shape[1]), 0).astype(f32)
        pick[e * CAP : (e + 1) * CAP, :] = one_hot(flat[e : e + 1, :] == j)
    loads[2].wait()
    packed_grads = dot(pick[...], hidden[...]).astype(bf16)
    j = lax.broadcasted_iota(jnp.int32, (CAP, per_token.shape[1]), 0)
    pick_acts = jnp.concatenate([one_hot(per_token[e : e + 1, :] == j) for e in range(experts)], axis=0)
    loads[1].wait()
    packed_acts = dot(pick_acts, acts[...]).astype(bf16)
    col = lax.broadcasted_iota(jnp.int32, (width, quarter), 1)
    origin = 8 * NY * (INNER * ((col >> 3) & (outer - 1)) + (col >> 6)) + (col & 7)
    row = lax.broadcasted_iota(jnp.int32, (width, quarter), 0)
    for q in range(NY):
        order = one_hot(row == origin + 8 * q)
        ordered = dot(packed_acts, order).astype(bf16)
        for e in range(experts):
            send[e, q, :, :quarter] = ordered[e * CAP : (e + 1) * CAP, :]
            send[e, q, :, quarter:] = packed_grads[e * CAP : (e + 1) * CAP, :]

    pl.semaphore_wait(barrier, group - 1 + 6)
    for dz in (4, -4):
        pl.semaphore_signal(know_four, inc=1, device_id=along(dz), device_id_type=MESH)

    def go(i):
        dy, do = offsets(i)
        return pltpu.make_async_remote_copy(
            src_ref=send.at[(opt + do) % n_opt, (y + dy) % NY],
            dst_ref=recv.at[i],
            send_sem=go_send.at[i],
            recv_sem=go_recv.at[i],
            device_id=go_peer(i),
            device_id_type=MESH,
        )

    def start_go(r, _):
        go(r).start()
        return 0

    lax.fori_loop(1, group, start_go, 0)
    own = pltpu.make_async_copy(send.at[opt, y], recv.at[0], local_sem)
    own.start()
    pl.semaphore_wait(know_four, 2)
    for dz in (8, -8):
        pl.semaphore_signal(know_eight, inc=1, device_id=along(dz), device_id_type=MESH)
    own.wait()

    def wait_go(r, _):
        go(r).wait_recv()
        return 0

    total = jnp.zeros((quarter, hid), f32)
    for chunk in range(NY):
        lax.fori_loop(max(1, chunk * n_opt), (chunk + 1) * n_opt, wait_go, 0)
        block = recv[chunk * n_opt : (chunk + 1) * n_opt].reshape(n_opt * CAP, quarter + hid)
        total = total + dot_t(block[:, :quarter], block[:, quarter:])
    part[...] = total.reshape(part.shape)

    steps = (1, INNER - 1, 2)
    nears = []
    for s in range(3):
        copy = pltpu.make_async_remote_copy(
            src_ref=part.at[(cls + steps[s]) % INNER],
            dst_ref=near.at[s],
            send_sem=near_send.at[s],
            recv_sem=near_recv.at[s],
            device_id=near_to[s],
            device_id_type=MESH,
        )
        copy.start()
        nears.append(copy)
    for copy in nears:
        copy.wait_recv()
    summed[...] = part[cls].reshape(summed.shape) + (
        near[0] + (near[1] + near[2])
    ).reshape(summed.shape)
    pl.semaphore_wait(know_eight, 2)
    fars = []
    for q in OFFSETS[:0:-1]:
        copy = pltpu.make_async_remote_copy(
            src_ref=summed.at[(place + q) % outer],
            dst_ref=far.at[q],
            send_sem=far_send.at[q],
            recv_sem=far_recv.at[q],
            device_id=far_to(q),
            device_id_type=MESH,
        )
        copy.start()
        fars.append(copy)
    loads[3].wait()
    loads[4].wait()
    grad = summed[place]
    for q, copy in zip(OFFSETS[1:], fars[::-1]):
        copy.wait_recv()
        grad = grad + far[q]
    moment = momentum_decay * momentum[...] + grad
    moment_out[...] = moment

    rows[0, 0] = moment
    outs = [None] * outer
    for i in range(outer - 1, 0, -1):
        outs[i] = pltpu.make_async_remote_copy(
            src_ref=rows.at[0, 0],
            dst_ref=rows.at[0, i],
            send_sem=out_send.at[i],
            recv_sem=out_recv.at[i],
            device_id=far_to(OFFSETS[i]),
            device_id_type=MESH,
        )
        outs[i].start()
    arounds, sides = {}, {}

    def to_sides(s, g):
        begin, end = GROUPS[g]
        for d in range(1, NY):
            slot = d * INNER + s
            sides[slot, g] = pltpu.make_async_remote_copy(
                src_ref=rows.at[s, begin:end],
                dst_ref=rows.at[slot, begin:end],
                send_sem=side_send.at[slot, g],
                recv_sem=side_recv.at[slot, g],
                device_id=at(z, (y + d) % NY, opt),
                device_id_type=MESH,
            )
            sides[slot, g].start()

    def from_places(g):
        begin, end = GROUPS[g]
        for i in range(max(begin, 1), end):
            outs[i].wait_recv()
        for s in range(1, INNER):
            arounds[s, g] = pltpu.make_async_remote_copy(
                src_ref=rows.at[0, begin:end],
                dst_ref=rows.at[s, begin:end],
                send_sem=around_send.at[s, g],
                recv_sem=around_recv.at[s, g],
                device_id=near_to[s - 1],
                device_id_type=MESH,
            )
            arounds[s, g].start()
        to_sides(0, g)

    def from_classes(g):
        for s in range(1, INNER):
            arounds[s, g].wait_recv()
            to_sides(s, g)

    last = len(GROUPS)
    for g in range(last + 1):
        if g < last:
            from_places(g)
        if g > 0:
            from_classes(g - 1)
    gram_hi = jnp.zeros((hid, hid), f32)
    gram_lo = jnp.zeros((hid, hid), f32)
    for g, (begin, end) in enumerate(GROUPS):
        for slot in range(INNER, NY * INNER):
            sides[slot, g].wait_recv()
        hi, lo = halves(rows[:, begin:end].reshape(NY * INNER * (end - begin) * 8, hid))
        gram_hi, gram_lo = gram_hi + dot_t(hi, hi), gram_lo + dot_t(hi, lo)

    gram = gram_hi + (gram_lo + gram_lo.T)
    eye = lax.broadcasted_iota(jnp.int32, gram.shape, 0) == lax.broadcasted_iota(jnp.int32, gram.shape, 1)
    scale = lax.rsqrt(jnp.sum(jnp.where(eye, gram, 0.0)) + norm_epsilon)
    one = jnp.where(eye, poly_first, 0.0)
    gram = gram * (scale * scale)
    gram_parts = halves(gram)
    first = one + (poly_third * gram + poly_fifth * dot3(gram_parts, gram_parts))
    first_parts = halves(first)
    later = dot3(first_parts, halves(dot3(gram_parts, first_parts)))
    later_parts = halves(later)
    second = one + (poly_third * later + poly_fifth * dot3(later_parts, later_parts))
    iterate = dot3(halves(dot3(halves(moment * scale), first_parts)), halves(second))
    update = 0.2 * math.sqrt(max(width, hid)) * iterate
    update_out[...] = update
    master_out[...] = (1.0 - learning_rate * weight_decay) * master[...] - learning_rate * update

    def wait_sent(i, _):
        go(i).wait_send()
        return 0

    lax.fori_loop(1, group, wait_sent, 0)
    for copy in nears + fars + outs[1:] + list(arounds.values()) + list(sides.values()):
        copy.wait_send()


def per_device(activations, hidden_grad, routing, momentum, master):
    n_opt = lax.axis_size("opt")
    nz = lax.axis_size("dp") // NY
    outer = nz // INNER
    tokens, width = activations.shape
    top, hid = hidden_grad.shape[1:]
    quarter = width // NY
    group = NY * n_opt
    dma = pltpu.SemaphoreType.DMA
    shape = jax.ShapeDtypeStruct(momentum.shape[1:], f32)
    vmem = pl.BlockSpec(memory_space=pltpu.VMEM)
    outs = pl.pallas_call(
        functools.partial(kernel, (nz, n_opt)),
        out_shape=(shape, shape, shape),
        in_specs=[pl.BlockSpec(memory_space=pltpu.HBM)] * 5,
        out_specs=(vmem, vmem, vmem),
        scratch_shapes=[
            pltpu.VMEM((tokens, width), bf16),
            pltpu.VMEM((tokens * top, hid), bf16),
            pltpu.VMEM((top, tokens), jnp.int32),
            pltpu.VMEM(shape.shape, f32),
            pltpu.VMEM(shape.shape, f32),
            pltpu.VMEM((n_opt * CAP, tokens * top), bf16),
            pltpu.VMEM((n_opt, NY, CAP, quarter + hid), bf16),
            pltpu.VMEM((group, CAP, quarter + hid), bf16),
            pltpu.VMEM((INNER, outer * 8, hid), f32),
            pltpu.VMEM((3, outer * 8, hid), f32),
            pltpu.VMEM((outer, 8, hid), f32),
            pltpu.VMEM((outer, 8, hid), f32),
            pltpu.VMEM((NY * INNER, outer, 8, hid), f32),
            dma((5,)),
            dma,
            pltpu.SemaphoreType.REGULAR,
            pltpu.SemaphoreType.REGULAR,
            dma((group,)), dma((group,)),
            dma((3,)), dma((3,)),
            dma((outer,)), dma((outer,)),
            dma((outer,)), dma((outer,)),
            dma((INNER, len(GROUPS))), dma((INNER, len(GROUPS))),
            dma((NY * INNER, len(GROUPS))), dma((NY * INNER, len(GROUPS))),
        ],
        compiler_params=pltpu.CompilerParams(
            collective_id=0, has_side_effects=True, vmem_limit_bytes=60 * 1024 * 1024
        ),
    )(
        activations,
        hidden_grad.reshape(tokens * top, hid),
        routing.T,
        momentum[0],
        master[0],
    )
    return tuple(out[None] for out in outs)


def solution(mesh):
    placed = (
        P(("dp", "opt"), None),
        P(("dp", "opt"), None, None),
        P(("dp", "opt"), None),
        P("opt", "dp", None),
        P("opt", "dp", None),
    )
    return jax.shard_map(
        per_device,
        mesh=mesh,
        in_specs=placed,
        out_specs=(P("opt", "dp", None), P("opt", "dp", None), P("opt", "dp", None)),
        check_vma=False,
    )
```

time: 854 us -> 103 us (0.12)
  the two profiles are of different devices: /device:TPU:2 before, /device:TPU:4 now
where the time goes in v1:
time: 103 us; the launch traced here: 102 us
  Pallas kernels  97.7 us (95%)
  local copies, waits for them, and re-layouts  3.92 us (4%)
    pallas_call x1, Pallas kernels, per_device(): pl.pallas_call(functools.partial(kernel, (nz, n_opt)), out_shape=(shape,...  97.7 us
    unnamed x3, local copies, waits for them, and re-layouts  3.92 us

profile of v1, /device:TPU:4, one launch (start us, length us, event | category | flops | bytes accessed | tf_op | source)
XLA Modules:
  0.0 102.3 jit_solution(2405439199265985619)
XLA Ops:
  0.6 97.7 %shard_map.76 = (f32[8,384]{1,0:T(8,128)}, f32[8,384]{1,0:T(8,128)}, f32[8,384]{1,0:T(8,128)}) custom-call(bf16[256,1024]{1,0:T(8,128)(2,1)} %acts_hbm.1, bf16[2048,384]{1,0:T(8,128)(2,1)} %bitcast.7, s32[8,256]{1,0:T(8,128)} %bitcast.13, f32[8,384]{1,0:T(8,128)} %bitcast.8, f32[8,384]{1,0:T(8,128)} %bitcast.9), custom_call_target="tpu_custom_call" | custom-call | tf_op jit(solution)/shard_map/pallas_call | solution.py:349
  98.4 1.3 %copy.11 = f32[1,8,384]{2,1,0:T(8,128)} copy(f32[1,8,384]{2,1,0:T(8,128)} %bitcast.12) | data formatting | bytes 24576
  99.7 1.3 %copy.12 = f32[1,8,384]{2,1,0:T(8,128)} copy(f32[1,8,384]{2,1,0:T(8,128)} %bitcast.11) | data formatting | bytes 24576
  101.0 1.3 %copy.13 = f32[1,8,384]{2,1,0:T(8,128)} copy(f32[1,8,384]{2,1,0:T(8,128)} %bitcast.10) | data formatting | bytes 24576

commit v2 on v1

--- a/solution.py
+++ b/solution.py
@@ -11,7 +11,7 @@
 CAP = 32
 NY = 4
 INNER = 4
-STRIDE = 11
+STRIDE = 5
 MESH = pl.DeviceIdType.MESH
 
 poly_first = 3.4445
@@ -46,6 +46,27 @@
 
 def one_hot(cond):
     return jnp.where(cond, 1.0, 0.0).astype(bf16)
+
+
+def step_of(exponent, mantissa):
+    return mantissa * (jnp.exp2(exponent - 14.0) * (1 / 32767))
+
+
+def coded(block):
+    peak = jnp.maximum(jnp.max(jnp.abs(block), keepdims=True), 1e-30)
+    exponent = jnp.floor(jnp.log(peak) * (1 / math.log(2)) + 0.001) + 1.0
+    mantissa = jnp.floor(peak * jnp.exp2(14.0 - exponent)) + 2.0
+    steps = jnp.round(block * (1.0 / step_of(exponent, mantissa)))
+    parts = [steps[:, c : c + 128] for c in range(0, block.shape[1], 128)]
+    first_half = lax.broadcasted_iota(jnp.int32, (8, 128), 0) < 4
+    parts.append(jnp.where(first_half, exponent, mantissa))
+    return jnp.concatenate(parts, axis=0).astype(jnp.int32).astype(jnp.int16)
+
+
+def decoded(blocks):
+    parts = blocks.astype(jnp.int32).astype(f32).reshape(-1, 4, 8, 128)
+    step = step_of(parts[:, 3, 0:1], parts[:, 3, 4:5])
+    return jnp.concatenate([(parts[:, c] * step).reshape(-1, 128) for c in range(3)], axis=1)
 
 
 def running_count(flags):
@@ -64,9 +85,9 @@
 
 def kernel(
     sizes,
-    acts_hbm, hidden_hbm, names_hbm, momentum_hbm, master_hbm,
-    moment_out, master_out, update_out,
-    acts, hidden, names, momentum, master,
+    acts_hbm, hidden_hbm, names_hbm, momentum_hbm,
+    result,
+    acts, hidden, names, momentum,
     pick, send, recv, part, near, summed, far, rows,
     load_sem, local_sem, know_four, know_eight,
     go_send, go_recv, near_send, near_recv, far_send, far_recv,
@@ -121,15 +142,15 @@
                 (acts_hbm, acts),
                 (hidden_hbm, hidden),
                 (momentum_hbm, momentum),
-                (master_hbm, master),
             ]
         )
     ]
-    for load in loads:
+    loads[0].start()
+    for dz in (4, -4, 2, -2, 1, -1):
+        pl.semaphore_signal(barrier, inc=1, device_id=along(dz), device_id_type=MESH)
+    for load in loads[1:]:
         load.start()
     lax.fori_loop(1, group, greet, 0)
-    for dz in (1, -1, 2, -2, 4, -4):
-        pl.semaphore_signal(barrier, inc=1, device_id=along(dz), device_id_type=MESH)
 
     experts, tokens, top = n_opt, acts.shape[0], names.shape[0]
     spread_shape = (tokens, tokens * top)
@@ -239,15 +260,14 @@
         copy.start()
         fars.append(copy)
     loads[3].wait()
-    loads[4].wait()
     grad = summed[place]
     for q, copy in zip(OFFSETS[1:], fars[::-1]):
         copy.wait_recv()
         grad = grad + far[q]
     moment = momentum_decay * momentum[...] + grad
-    moment_out[...] = moment
-
-    rows[0, 0] = moment
+    result[0] = moment
+
+    rows[0, 0] = coded(moment)
     outs = [None] * outer
     for i in range(outer - 1, 0, -1):
         outs[i] = pltpu.make_async_remote_copy(
@@ -307,7 +327,7 @@
     for g, (begin, end) in enumerate(GROUPS):
         for slot in range(INNER, NY * INNER):
             sides[slot, g].wait_recv()
-        hi, lo = halves(rows[:, begin:end].reshape(NY * INNER * (end - begin) * 8, hid))
+        hi, lo = halves(decoded(rows[:, begin:end]))
         gram_hi, gram_lo = gram_hi + dot_t(hi, hi), gram_lo + dot_t(hi, lo)
 
     gram = gram_hi + (gram_lo + gram_lo.T)
@@ -321,10 +341,7 @@
     later = dot3(first_parts, halves(dot3(gram_parts, first_parts)))
     later_parts = halves(later)
     second = one + (poly_third * later + poly_fifth * dot3(later_parts, later_parts))
-    iterate = dot3(halves(dot3(halves(moment * scale), first_parts)), halves(second))
-    update = 0.2 * math.sqrt(max(width, hid)) * iterate
-    update_out[...] = update
-    master_out[...] = (1.0 - learning_rate * weight_decay) * master[...] - learning_rate * update
+    result[1] = dot3(halves(dot3(halves(moment * scale), first_parts)), halves(second))
 
     def wait_sent(i, _):
         go(i).wait_send()
@@ -346,16 +363,15 @@
     dma = pltpu.SemaphoreType.DMA
     shape = jax.ShapeDtypeStruct(momentum.shape[1:], f32)
     vmem = pl.BlockSpec(memory_space=pltpu.VMEM)
-    outs = pl.pallas_call(
+    result = pl.pallas_call(
         functools.partial(kernel, (nz, n_opt)),
-        out_shape=(shape, shape, shape),
-        in_specs=[pl.BlockSpec(memory_space=pltpu.HBM)] * 5,
-        out_specs=(vmem, vmem, vmem),
+        out_shape=jax.ShapeDtypeStruct((2, *shape.shape), f32),
+        in_specs=[pl.BlockSpec(memory_space=pltpu.HBM)] * 4,
+        out_specs=vmem,
         scratch_shapes=[
             pltpu.VMEM((tokens, width), bf16),
             pltpu.VMEM((tokens * top, hid), bf16),
             pltpu.VMEM((top, tokens), jnp.int32),
-            pltpu.VMEM(shape.shape, f32),
             pltpu.VMEM(shape.shape, f32),
             pltpu.VMEM((n_opt * CAP, tokens * top), bf16),
             pltpu.VMEM((n_opt, NY, CAP, quarter + hid), bf16),
@@ -364,8 +380,8 @@
             pltpu.VMEM((3, outer * 8, hid), f32),
             pltpu.VMEM((outer, 8, hid), f32),
             pltpu.VMEM((outer, 8, hid), f32),
-            pltpu.VMEM((NY * INNER, outer, 8, hid), f32),
-            dma((5,)),
+            pltpu.VMEM((NY * INNER, outer, 32, 128), jnp.int16),
+            dma((4,)),
             dma,
             pltpu.SemaphoreType.REGULAR,
             pltpu.SemaphoreType.REGULAR,
@@ -384,9 +400,11 @@
         hidden_grad.reshape(tokens * top, hid),
         routing.T,
         momentum[0],
-        master[0],
     )
-    return tuple(out[None] for out in outs)
+    new_moment, iterate = result[:1], result[1:]
+    update = 0.2 * math.sqrt(max(width, hid)) * iterate
+    master_out = (1.0 - learning_rate * weight_decay) * master - learning_rate * update
+    return (new_moment, master_out, update)
 
 
 def solution(mesh):

time: 103 us -> 92.2 us (0.90)
  the two profiles are of different devices: /device:TPU:4 before, /device:TPU:32 now
where the time goes in v2:
time: 92.2 us; the launch traced here: 92 us
  Pallas kernels  90 us (98%)
  other arithmetic  1.34 us (1%)
    pallas_call x1, Pallas kernels, per_device(): pl.pallas_call(functools.partial(kernel, (nz, n_opt)), out_shape=jax.Shap...  90 us

profile of v2, /device:TPU:32, one launch (start us, length us, event | category | flops | bytes accessed | tf_op | source)
XLA Modules:
  0.0 92.0 jit_solution(17638621241917211438)
XLA Ops:
  0.6 0.0 copy-start
  0.6 90.0 %shard_map.76 = f32[2,8,384]{2,1,0:T(8,128)} custom-call(bf16[256,1024]{1,0:T(8,128)(2,1)} %acts_hbm.1, bf16[2048,384]{1,0:T(8,128)(2,1)} %bitcast.3, s32[8,256]{1,0:T(8,128)} %bitcast.5, f32[8,384]{1,0:T(8,128)} %bitcast.4), custom_call_target="tpu_custom_call" | custom-call | tf_op jit(solution)/shard_map/pallas_call | solution.py:366
  90.7 0.0 copy-done
  90.7 1.3 %slice_multiply_fusion = (f32[1,8,384]{2,1,0:T(8,128)}, f32[1,8,384]{2,1,0:T(8,128)}, f32[1,8,384]{2,1,0:T(8,128)}) fusion(f32[2,8,384]{2,1,0:T(8,128)} %shard_map.76, f32[1,8,384]{2,1,0:T(8,128)S(1)} %copy-done), kind=kLoop, calls=%fused_computation.1 | loop fusion | flops 12288 | bytes 73728 | tf_op jit(solution)/shard_map/mul | solution.py:405
Async XLA Ops:
  0.6 90.0 %copy-start = (f32[1,8,384]{2,1,0:T(8,128)S(1)}, f32[1,8,384]{2,1,0:T(8,128)}, u32[]{:S(2)}) copy-start(f32[1,8,384]{2,1,0:T(8,128)} %param.9) | copy-start | bytes 36868

commit v3 on v2

--- a/solution.py
+++ b/solution.py
@@ -114,10 +114,6 @@
         dy, do = offsets(i)
         return at(z, (y + dy) % NY, (opt + do) % n_opt)
 
-    def go_source(i):
-        dy, do = offsets(i)
-        return at(z, (y + NY - dy) % NY, (opt + n_opt - do) % n_opt)
-
     def along(dz):
         return at((z + nz + dz) % nz, y, opt)
 
@@ -131,7 +127,8 @@
     barrier = pltpu.get_barrier_semaphore()
 
     def greet(i, _):
-        pl.semaphore_signal(barrier, inc=1, device_id=go_source(i), device_id_type=MESH)
+        target = at(z, (y + NY // 2 + i // n_opt) % NY, (opt + n_opt // 2 + i % n_opt) % n_opt)
+        pl.semaphore_signal(barrier, inc=1, device_id=target, device_id_type=MESH)
         return 0
 
     loads = [
@@ -145,12 +142,16 @@
             ]
         )
     ]
+    own = NY // 2 * n_opt + n_opt // 2
     loads[0].start()
-    for dz in (4, -4, 2, -2, 1, -1):
+    for dz in (4, -4):
         pl.semaphore_signal(barrier, inc=1, device_id=along(dz), device_id_type=MESH)
+    lax.fori_loop(0, own, greet, 0)
     for load in loads[1:]:
         load.start()
-    lax.fori_loop(1, group, greet, 0)
+    lax.fori_loop(own + 1, group, greet, 0)
+    for dz in (2, -2, 1, -1):
+        pl.semaphore_signal(barrier, inc=1, device_id=along(dz), device_id_type=MESH)
 
     experts, tokens, top = n_opt, acts.shape[0], names.shape[0]
     spread_shape = (tokens, tokens * top)
@@ -180,20 +181,26 @@
     pick_acts = jnp.concatenate([one_hot(per_token[e : e + 1, :] == j) for e in range(experts)], axis=0)
     loads[1].wait()
     packed_acts = dot(pick_acts, acts[...]).astype(bf16)
-    col = lax.broadcasted_iota(jnp.int32, (width, quarter), 1)
-    origin = 8 * NY * (INNER * ((col >> 3) & (outer - 1)) + (col >> 6)) + (col & 7)
-    row = lax.broadcasted_iota(jnp.int32, (width, quarter), 0)
+    parts = []
+    row = lax.broadcasted_iota(jnp.int32, (quarter, quarter), 0)
+    lane = lax.broadcasted_iota(jnp.int32, (quarter, quarter), 1)
+    in_class = (((lane >> 3) & 1) * INNER + ((lane >> 4) & 3)) * (8 * NY) + (lane & 7)
+    for i in range(NY):
+        origin = in_class + ((((lane >> 6) + (NY - i)) & (NY - 1)) << 3)
+        ordered = dot(packed_acts[:, i * quarter : (i + 1) * quarter], one_hot(row == origin))
+        parts.append(ordered)
+    low = (lax.broadcasted_iota(jnp.int32, (n_opt * CAP, 128), 1) & 64) == 0
     for q in range(NY):
-        order = one_hot(row == origin + 8 * q)
-        ordered = dot(packed_acts, order).astype(bf16)
+        for half in range(2):
+            lanes = slice(128 * half, 128 * half + 128)
+            pieces = [parts[(2 * half + k + NY - q) % NY][:, lanes] for k in range(2)]
+            piece = jnp.where(low, pieces[0], pieces[1]).astype(bf16)
+            for e in range(experts):
+                send[e, q, :, lanes] = piece[e * CAP : (e + 1) * CAP, :]
         for e in range(experts):
-            send[e, q, :, :quarter] = ordered[e * CAP : (e + 1) * CAP, :]
             send[e, q, :, quarter:] = packed_grads[e * CAP : (e + 1) * CAP, :]
 
     pl.semaphore_wait(barrier, group - 1 + 6)
-    for dz in (4, -4):
-        pl.semaphore_signal(know_four, inc=1, device_id=along(dz), device_id_type=MESH)
-
     def go(i):
         dy, do = offsets(i)
         return pltpu.make_async_remote_copy(
@@ -210,6 +217,8 @@
         return 0
 
     lax.fori_loop(1, group, start_go, 0)
+    for dz in (4, -4):
+        pl.semaphore_signal(know_four, inc=1, device_id=along(dz), device_id_type=MESH)
     own = pltpu.make_async_copy(send.at[opt, y], recv.at[0], local_sem)
     own.start()
     pl.semaphore_wait(know_four, 2)
@@ -222,11 +231,15 @@
         return 0
 
     total = jnp.zeros((quarter, hid), f32)
-    for chunk in range(NY):
-        lax.fori_loop(max(1, chunk * n_opt), (chunk + 1) * n_opt, wait_go, 0)
-        block = recv[chunk * n_opt : (chunk + 1) * n_opt].reshape(n_opt * CAP, quarter + hid)
+    for begin, end in ((0, 8), (8, 16), (16, 24), (24, 28), (28, 32)):
+        lax.fori_loop(max(1, begin), end, wait_go, 0)
+        block = recv[begin:end].reshape((end - begin) * CAP, quarter + hid)
         total = total + dot_t(block[:, :quarter], block[:, quarter:])
-    part[...] = total.reshape(part.shape)
+    for p in range(NY):
+        for c in range(INNER):
+            rows_at = p * 64 + c * 16
+            pair = pl.ds(2 * ((p + NY - y) % NY), 2)
+            part[c, pair] = total[rows_at : rows_at + 16].reshape(2, 8, hid)
 
     steps = (1, INNER - 1, 2)
     nears = []
@@ -243,9 +256,7 @@
         nears.append(copy)
     for copy in nears:
         copy.wait_recv()
-    summed[...] = part[cls].reshape(summed.shape) + (
-        near[0] + (near[1] + near[2])
-    ).reshape(summed.shape)
+    summed[...] = part[cls] + (near[0] + (near[1] + near[2]))
     pl.semaphore_wait(know_eight, 2)
     fars = []
     for q in OFFSETS[:0:-1]:
@@ -376,8 +387,8 @@
             pltpu.VMEM((n_opt * CAP, tokens * top), bf16),
             pltpu.VMEM((n_opt, NY, CAP, quarter + hid), bf16),
             pltpu.VMEM((group, CAP, quarter + hid), bf16),
-            pltpu.VMEM((INNER, outer * 8, hid), f32),
-            pltpu.VMEM((3, outer * 8, hid), f32),
+            pltpu.VMEM((INNER, outer, 8, hid), f32),
+            pltpu.VMEM((3, outer, 8, hid), f32),
             pltpu.VMEM((outer, 8, hid), f32),
             pltpu.VMEM((outer, 8, hid), f32),
             pltpu.VMEM((NY * INNER, outer, 32, 128), jnp.int16),

time: 92.2 us -> 91.6 us (level)
  no operation moved by 1% of the time
where the time goes in v3:
time: 91.6 us; the launch traced here: 91.4 us
  Pallas kernels  89.4 us (98%)
  other arithmetic  1.34 us (1%)
    pallas_call x1, Pallas kernels, per_device(): pl.pallas_call(functools.partial(kernel, (nz, n_opt)), out_shape=jax.Shap...  89.4 us

profile of v3, /device:TPU:32, one launch (start us, length us, event | category | flops | bytes accessed | tf_op | source)
XLA Modules:
  0.0 91.4 jit_solution(2146691825897881136)
XLA Ops:
  0.6 0.0 copy-start
  0.6 89.4 %shard_map.76 = f32[2,8,384]{2,1,0:T(8,128)} custom-call(bf16[256,1024]{1,0:T(8,128)(2,1)} %acts_hbm.1, bf16[2048,384]{1,0:T(8,128)(2,1)} %bitcast.3, s32[8,256]{1,0:T(8,128)} %bitcast.5, f32[8,384]{1,0:T(8,128)} %bitcast.4), custom_call_target="tpu_custom_call" | custom-call | tf_op jit(solution)/shard_map/pallas_call | solution.py:377
  90.0 0.0 copy-done
  90.0 1.3 %slice_multiply_fusion = (f32[1,8,384]{2,1,0:T(8,128)}, f32[1,8,384]{2,1,0:T(8,128)}, f32[1,8,384]{2,1,0:T(8,128)}) fusion(f32[2,8,384]{2,1,0:T(8,128)} %shard_map.76, f32[1,8,384]{2,1,0:T(8,128)S(1)} %copy-done), kind=kLoop, calls=%fused_computation.1 | loop fusion | flops 12288 | bytes 73728 | tf_op jit(solution)/shard_map/mul | solution.py:416
Async XLA Ops:
  0.6 89.4 %copy-start = (f32[1,8,384]{2,1,0:T(8,128)S(1)}, f32[1,8,384]{2,1,0:T(8,128)}, u32[]{:S(2)}) copy-start(f32[1,8,384]{2,1,0:T(8,128)} %param.9) | copy-start | bytes 36868

commit v4 on v3

--- a/solution.py
+++ b/solution.py
@@ -81,6 +81,7 @@
 
 OFFSETS = (0, 1, 7, 2, 6, 3, 5, 4)
 GROUPS = ((0, 3), (3, 5), (5, 8))
+COLUMNS = (slice(0, 256), slice(256, 384))
 
 
 def kernel(
@@ -242,38 +243,40 @@
             part[c, pair] = total[rows_at : rows_at + 16].reshape(2, 8, hid)
 
     steps = (1, INNER - 1, 2)
-    nears = []
-    for s in range(3):
-        copy = pltpu.make_async_remote_copy(
-            src_ref=part.at[(cls + steps[s]) % INNER],
-            dst_ref=near.at[s],
-            send_sem=near_send.at[s],
-            recv_sem=near_recv.at[s],
-            device_id=near_to[s],
-            device_id_type=MESH,
+    nears, fars = {}, {}
+    for h, cols in enumerate(COLUMNS):
+        for s in range(3):
+            nears[h, s] = pltpu.make_async_remote_copy(
+                src_ref=part.at[(cls + steps[s]) % INNER, :, :, cols],
+                dst_ref=near.at[s, :, :, cols],
+                send_sem=near_send.at[h, s],
+                recv_sem=near_recv.at[h, s],
+                device_id=near_to[s],
+                device_id_type=MESH,
+            )
+            nears[h, s].start()
+    pl.semaphore_wait(know_eight, 2)
+    for h, cols in enumerate(COLUMNS):
+        for s in range(3):
+            nears[h, s].wait_recv()
+        summed[:, :, cols] = part[cls, :, :, cols] + (
+            near[0, :, :, cols] + (near[1, :, :, cols] + near[2, :, :, cols])
         )
-        copy.start()
-        nears.append(copy)
-    for copy in nears:
-        copy.wait_recv()
-    summed[...] = part[cls] + (near[0] + (near[1] + near[2]))
-    pl.semaphore_wait(know_eight, 2)
-    fars = []
-    for q in OFFSETS[:0:-1]:
-        copy = pltpu.make_async_remote_copy(
-            src_ref=summed.at[(place + q) % outer],
-            dst_ref=far.at[q],
-            send_sem=far_send.at[q],
-            recv_sem=far_recv.at[q],
-            device_id=far_to(q),
-            device_id_type=MESH,
-        )
-        copy.start()
-        fars.append(copy)
+        for q in OFFSETS[:0:-1]:
+            fars[h, q] = pltpu.make_async_remote_copy(
+                src_ref=summed.at[(place + q) % outer, :, cols],
+                dst_ref=far.at[q, :, cols],
+                send_sem=far_send.at[h, q],
+                recv_sem=far_recv.at[h, q],
+                device_id=far_to(q),
+                device_id_type=MESH,
+            )
+            fars[h, q].start()
     loads[3].wait()
     grad = summed[place]
-    for q, copy in zip(OFFSETS[1:], fars[::-1]):
-        copy.wait_recv()
+    for q in OFFSETS[1:]:
+        for h in range(len(COLUMNS)):
+            fars[h, q].wait_recv()
         grad = grad + far[q]
     moment = momentum_decay * momentum[...] + grad
     result[0] = moment
@@ -359,7 +362,7 @@
         return 0
 
     lax.fori_loop(1, group, wait_sent, 0)
-    for copy in nears + fars + outs[1:] + list(arounds.values()) + list(sides.values()):
+    for copy in [*nears.values(), *fars.values(), *outs[1:], *arounds.values(), *sides.values()]:
         copy.wait_send()
 
 
@@ -397,8 +400,8 @@
             pltpu.SemaphoreType.REGULAR,
             pltpu.SemaphoreType.REGULAR,
             dma((group,)), dma((group,)),
-            dma((3,)), dma((3,)),
-            dma((outer,)), dma((outer,)),
+            dma((len(COLUMNS), 3)), dma((len(COLUMNS), 3)),
+            dma((len(COLUMNS), outer)), dma((len(COLUMNS), outer)),
             dma((outer,)), dma((outer,)),
             dma((INNER, len(GROUPS))), dma((INNER, len(GROUPS))),
             dma((NY * INNER, len(GROUPS))), dma((NY * INNER, len(GROUPS))),

time: 91.6 us -> 92.4 us (level)
  no operation moved by 1% of the time
where the time goes in v4:
time: 92.4 us; the launch traced here: 92.2 us
  Pallas kernels  90.2 us (98%)
  other arithmetic  1.34 us (1%)
    pallas_call x1, Pallas kernels, per_device(): pl.pallas_call(functools.partial(kernel, (nz, n_opt)), out_shape=jax.Shap...  90.2 us

profile of v4, /device:TPU:32, one launch (start us, length us, event | category | flops | bytes accessed | tf_op | source)
XLA Modules:
  0.0 92.2 jit_solution(12491840893357623373)
XLA Ops:
  0.6 0.0 copy-start
  0.6 90.2 %shard_map.76 = f32[2,8,384]{2,1,0:T(8,128)} custom-call(bf16[256,1024]{1,0:T(8,128)(2,1)} %acts_hbm.1, bf16[2048,384]{1,0:T(8,128)(2,1)} %bitcast.3, s32[8,256]{1,0:T(8,128)} %bitcast.5, f32[8,384]{1,0:T(8,128)} %bitcast.4), custom_call_target="tpu_custom_call" | custom-call | tf_op jit(solution)/shard_map/pallas_call | solution.py:380
  90.8 0.0 copy-done
  90.8 1.3 %slice_multiply_fusion = (f32[1,8,384]{2,1,0:T(8,128)}, f32[1,8,384]{2,1,0:T(8,128)}, f32[1,8,384]{2,1,0:T(8,128)}) fusion(f32[2,8,384]{2,1,0:T(8,128)} %shard_map.76, f32[1,8,384]{2,1,0:T(8,128)S(1)} %copy-done), kind=kLoop, calls=%fused_computation.1 | loop fusion | flops 12288 | bytes 73728 | tf_op jit(solution)/shard_map/mul | solution.py:419
Async XLA Ops:
  0.6 90.2 %copy-start = (f32[1,8,384]{2,1,0:T(8,128)S(1)}, f32[1,8,384]{2,1,0:T(8,128)}, u32[]{:S(2)}) copy-start(f32[1,8,384]{2,1,0:T(8,128)} %param.9) | copy-start | bytes 36868
